TPU v7x, 512 devices: a whole 4x4x16 slice. The times are simulated.
512 devices in a mesh: blk: 8 (over y, x_hi), grp: 64 (over z, x_lo, core).
Axes of the slice: x: 4 (x_hi: 2, x_lo: 2; x = x_hi * 2 + x_lo), y: 4, z: 16, core: 2. Of those that a mesh axis runs over, the one named last changes fastest.
Arguments:
- image_embed: bfloat16 [6144, 1152], P(('blk', 'grp')), may hold values from -1 to 1
- text_embed: bfloat16 [6144, 1152], P(('blk', 'grp')), may hold values from -1 to 1
- logit_scale: float32 [], replicated, may hold values from 4 to 10
- logit_bias: float32 [], replicated, may hold values from -6 to -2
Outputs:
- image_grad: float32 [6144, 1152], P(('blk', 'grp'))
- text_grad: float32 [6144, 1152], P(('blk', 'grp'))
All inputs are finite; a program needn't handle non-finite values.
Results may differ from a plain program's by a relative error of at most 0.0055.
Values may be sent and summed in bfloat16 or wider, within the bound.
A program may use at most 64 MiB of HBM per device.

v0:
```python
import jax
import jax.numpy as jnp
from jax import lax
from jax.sharding import PartitionSpec as P

EPS = 1e-06


def from_behind(block, axis, distance):
    devices = range(lax.axis_size(axis))
    route = [((i - distance) % len(devices), i) for i in devices]
    return lax.ppermute(block, axis, route)


def unit_rows(embed):
    values = embed.astype(jnp.float32)
    recip = lax.rsqrt(jnp.sum(values * values, axis=1, keepdims=True) + EPS)
    unit = values * recip
    return (unit, unit.astype(jnp.bfloat16), recip)


def back_norm(unit, recip, grad):
    return recip * (grad - unit * jnp.sum(unit * grad, axis=1, keepdims=True))


def shards(image_embed, text_embed, logit_scale, logit_bias):
    image_unit, image_half, image_recip = unit_rows(image_embed)
    text_unit, text_half, text_recip = unit_rows(text_embed)
    rows = image_half.shape[0]
    width = image_half.shape[1]
    n_blk = lax.axis_size("blk")
    home = lax.axis_index("blk")
    member = lax.axis_index("grp")
    text_block = lax.all_gather(text_half, "grp", axis=0, tiled=True)
    span = text_block.shape[0]
    row_ids = lax.broadcasted_iota(jnp.int32, (rows, span), 0)
    col_ids = lax.broadcasted_iota(jnp.int32, (rows, span), 1)
    on_diagonal = col_ids == member * rows + row_ids
    coefs = []
    visits = []

    def record(visit, anchor, total):
        logits = (
            logit_scale
            * lax.dot_general(
                visit, text_block, (((1,), (1,)), ((), ())), preferred_element_type=jnp.float32
            )
            + logit_bias
        )
        positive = jnp.logical_and(on_diagonal, anchor == home)
        coef = jnp.where(positive, -jax.nn.sigmoid(-logits), jax.nn.sigmoid(logits)).astype(
            jnp.bfloat16
        )
        grad = logit_scale * jnp.dot(coef, text_block, preferred_element_type=jnp.float32)
        coefs.append(coef)
        visits.append(visit)
        total = total + logit_scale * lax.dot_general(
            coef, visit, (((0,), (0,)), ((), ())), preferred_element_type=jnp.float32
        )
        return (grad, total)

    text_total = jnp.zeros((span, width), jnp.float32)
    visit = image_half
    carried = jnp.zeros((rows, width), jnp.float32)
    for step in range(n_blk):
        if step > 0:
            sent, carried = from_behind((visit.astype(jnp.float32), carried), "blk", 1)
            visit = sent.astype(jnp.bfloat16)
        grad, text_total = record(visit, (home - step) % n_blk, text_total)
        carried = carried + grad
    image_unit_grad = from_behind(carried, "blk", 1)
    text_unit_grad = lax.psum_scatter(text_total, "grp", scatter_dimension=0, tiled=True)
    return (
        back_norm(image_unit, image_recip, image_unit_grad),
        back_norm(text_unit, text_recip, text_unit_grad),
    )


def solution(mesh):
    return jax.shard_map(
        shards,
        mesh=mesh,
        in_specs=(P(("blk", "grp"), None), P(("blk", "grp"), None), P(), P()),
        out_specs=(P(("blk", "grp"), None), P(("blk", "grp"), None)),
        check_vma=False,
    )
```

profile of v0, /device:TPU:1, one launch (start us, length us, event | category | flops | bytes accessed | tf_op | source)
XLA Modules:
  0.0 404.8 jit_solution(5549938715707711281)
XLA Ops:
  11.3 5.5 %collective-permute-start.1 = (bf16[12,1152]{1,0:T(8,128)(2,1)S(1)}, bf16[12,1152]{1,0:T(8,128)(2,1)S(1)}, u32[]{:S(2)}, u32[]{:S(2)}) collective-permute-start(bf16[12,1152]{1,0:T(8,128)(2,1)S(1)} %fusion.60), channel_id=1, source_target_pairs={{448,0},{0,64},{64,128},{128,192},{192,256},{256,320},{320,384},{3... | collective-permute-start | bytes 82952 | tf_op jit(solution)/shard_map/ppermute | solution.py:12
  16.8 3.8 collective-permute-done.1
  20.6 2.4 collective-permute-start.3
  23.0 5.9 %collective-permute-done.3 = bf16[12,1152]{1,0:T(8,128)(2,1)S(1)} collective-permute-done((bf16[12,1152]{1,0:T(8,128)(2,1)S(1)}, bf16[12,1152]{1,0:T(8,128)(2,1)S(1)}, u32[]{:S(2)}, u32[]{:S(2)}) %collective-permute-start.3) | collective-permute-done | bytes 27680 | tf_op jit(solution)/shard_map/ppermute | solution.py:12
  30.8 6.4 %collective-permute-done.5 = bf16[12,1152]{1,0:T(8,128)(2,1)S(1)} collective-permute-done((bf16[12,1152]{1,0:T(8,128)(2,1)S(1)}, bf16[12,1152]{1,0:T(8,128)(2,1)S(1)}, u32[]{:S(2)}, u32[]{:S(2)}) %collective-permute-start.5) | collective-permute-done | bytes 27680 | tf_op jit(solution)/shard_map/ppermute | solution.py:12
  39.1 6.8 %collective-permute-done.7 = bf16[12,1152]{1,0:T(8,128)(2,1)S(1)} collective-permute-done((bf16[12,1152]{1,0:T(8,128)(2,1)S(1)}, bf16[12,1152]{1,0:T(8,128)(2,1)S(1)}, u32[]{:S(2)}, u32[]{:S(2)}) %collective-permute-start.7) | collective-permute-done | bytes 27680 | tf_op jit(solution)/shard_map/ppermute | solution.py:12
  47.8 6.6 %collective-permute-done.9 = bf16[12,1152]{1,0:T(8,128)(2,1)S(1)} collective-permute-done((bf16[12,1152]{1,0:T(8,128)(2,1)S(1)}, bf16[12,1152]{1,0:T(8,128)(2,1)S(1)}, u32[]{:S(2)}, u32[]{:S(2)}) %collective-permute-start.9) | collective-permute-done | bytes 27680 | tf_op jit(solution)/shard_map/ppermute | solution.py:12
  59.7 3.0 collective-permute-done.11
  64.6 74.7 %all-gather.3.cloned.1.call-done = bf16[64,12,1152]{2,1,0:T(8,128)(2,1)} async-done(((bf16[1,12,1152]{2,1,0:T(8,128)(2,1)}), bf16[64,12,1152]{2,1,0:T(8,128)(2,1)}) %all-gather.3.cloned.1.call-update) | async-done | bytes 1769488 | tf_op jit(solution)/shard_map/all_gather | solution.py:34
  139.4 2.5 reshape.19
  143.6 4.2 %collective-permute-start = (f32[12,1152]{1,0:T(8,128)S(1)}, f32[12,1152]{1,0:T(8,128)S(1)}, u32[]{:S(2)}, u32[]{:S(2)}) collective-permute-start(f32[12,1152]{1,0:T(8,128)S(1)} %convolution_multiply_fusion.7), channel_id=1, source_target_pairs={{448,0},{0,64},{64,128},{128,192},{192,256},{256,320},{320,384},{3... | collective-permute-start | bytes 165896 | tf_op jit(solution)/shard_map/ppermute | solution.py:12
  156.1 3.2 fusion.6
  159.3 128.7 %fusion = f32[16,1152]{1,0:T(8,128)S(1)} fusion(f32[768,1152]{1,0:T(8,128)} %fusion.6), kind=kCustom, calls=%all-reduce-scatter | all-reduce-scatter fusion | flops 1179649 | bytes 3614720
  288.4 4.7 %collective-permute-start.2 = (f32[12,1152]{1,0:T(8,128)S(1)}, f32[12,1152]{1,0:T(8,128)S(1)}, u32[]{:S(2)}, u32[]{:S(2)}) collective-permute-start(f32[12,1152]{1,0:T(8,128)S(1)} %fusion.7), channel_id=1, source_target_pairs={{448,0},{0,64},{64,128},{128,192},{192,256},{256,320},{320,384},{3... | collective-permute-start | bytes 165896 | tf_op jit(solution)/shard_map/ppermute | solution.py:12
  293.4 3.7 collective-permute-done.2
  297.1 2.6 collective-permute-start.4
  300.0 8.7 %collective-permute-start.29 = (f32[16,1152]{1,0:T(8,128)S(1)}, f32[16,1152]{1,0:T(8,128)S(1)}, u32[]{:S(2)}, u32[]{:S(2)}) collective-permute-start(f32[16,1152]{1,0:T(8,128)S(1)} %fusion), channel_id=1, source_target_pairs={{0,15},{1,16},{2,17},{3,18},{4,19},{5,20},{6,21},{7,22},{8,23},{9,... | collective-permute-start | bytes 221192
  310.1 5.4 %collective-permute-start.30 = (f32[12,1152]{1,0:T(8,128)S(1)}, f32[12,1152]{1,0:T(8,128)S(1)}, u32[]{:S(2)}, u32[]{:S(2)}) collective-permute-start(f32[12,1152]{1,0:T(8,128)S(1)} %slice), channel_id=1, source_target_pairs={{0,16},{1,17},{2,18},{3,19},{4,20},{5,21},{6,22},{7,23},{8,24},{9,... | collective-permute-start | bytes 165896
  315.5 4.8 %collective-permute-start.6 = (f32[12,1152]{1,0:T(8,128)S(1)}, f32[12,1152]{1,0:T(8,128)S(1)}, u32[]{:S(2)}, u32[]{:S(2)}) collective-permute-start(f32[12,1152]{1,0:T(8,128)S(1)} %add.204), channel_id=1, source_target_pairs={{448,0},{0,64},{64,128},{128,192},{192,256},{256,320},{320,384},{3... | collective-permute-start | bytes 165896 | tf_op jit(solution)/shard_map/ppermute | solution.py:12
  322.0 2.5 collective-permute-done.6
  327.1 9.7 %collective-permute-start.24 = (f32[16,1152]{1,0:T(8,128)S(1)}, f32[16,1152]{1,0:T(8,128)S(1)}, u32[]{:S(2)}, u32[]{:S(2)}) collective-permute-start(f32[16,1152]{1,0:T(8,128)S(1)} %fusion), channel_id=1, source_target_pairs={{0,10},{1,11},{2,12},{3,13},{4,14},{5,15},{6,16},{7,17},{8,18},{9,... | collective-permute-start | bytes 221192
  336.8 2.8 collective-permute-start.8
  343.6 8.8 %collective-permute-start.21 = (f32[16,1152]{1,0:T(8,128)S(1)}, f32[16,1152]{1,0:T(8,128)S(1)}, u32[]{:S(2)}, u32[]{:S(2)}) collective-permute-start(f32[16,1152]{1,0:T(8,128)S(1)} %fusion), channel_id=1, source_target_pairs={{0,7},{1,8},{2,9},{3,10},{4,11},{5,12},{6,13},{7,14},{8,15},{9,16}... | collective-permute-start | bytes 221192
  352.4 3.3 collective-permute-start.20
  355.7 2.8 collective-permute-start.19
  359.0 3.4 collective-permute-start.18
  363.7 3.1 collective-permute-start.16
  366.8 3.1 collective-permute-start.15
  372.2 2.2 concatenate
  374.5 5.1 %collective-permute-done.10 = f32[12,1152]{1,0:T(8,128)S(1)} collective-permute-done((f32[12,1152]{1,0:T(8,128)S(1)}, f32[12,1152]{1,0:T(8,128)S(1)}, u32[]{:S(2)}, u32[]{:S(2)}) %collective-permute-start.10) | collective-permute-done | bytes 55328 | tf_op jit(solution)/shard_map/ppermute | solution.py:12
  381.7 6.6 %collective-permute-done.12 = f32[12,1152]{1,0:T(8,128)S(1)} collective-permute-done((f32[12,1152]{1,0:T(8,128)S(1)}, f32[12,1152]{1,0:T(8,128)S(1)}, u32[]{:S(2)}, u32[]{:S(2)}) %collective-permute-start.12) | collective-permute-done | bytes 55328 | tf_op jit(solution)/shard_map/ppermute | solution.py:12
  391.0 6.1 %collective-permute-done.14 = f32[12,1152]{1,0:T(8,128)S(1)} collective-permute-done((f32[12,1152]{1,0:T(8,128)S(1)}, f32[12,1152]{1,0:T(8,128)S(1)}, u32[]{:S(2)}, u32[]{:S(2)}) %collective-permute-start.14) | collective-permute-done | bytes 55328 | tf_op jit(solution)/shard_map/ppermute | solution.py:12
  (83 shorter events, 45.0 us)
Async XLA Ops:
  7.2 132.2 %all-gather.3.cloned.1.call-start = ((), (), s32[]{:S(2)}) async-start(), calls=%async_computation | async-start | bytes 2396160 | tf_op jit(solution)/shard_map/all_gather | solution.py:34
  11.3 9.3 %collective-permute-start.1 = (bf16[12,1152]{1,0:T(8,128)(2,1)S(1)}, bf16[12,1152]{1,0:T(8,128)(2,1)S(1)}, u32[]{:S(2)}, u32[]{:S(2)}) collective-permute-start(bf16[12,1152]{1,0:T(8,128)(2,1)S(1)} %fusion.60), channel_id=1, source_target_pairs={{448,0},{0,64},{64,128},{128,192},{192,256},{256,320},{320,384},{3... | collective-permute-start | bytes 82952 | tf_op jit(solution)/shard_map/ppermute | solution.py:12
  20.6 8.3 %collective-permute-start.3 = (bf16[12,1152]{1,0:T(8,128)(2,1)S(1)}, bf16[12,1152]{1,0:T(8,128)(2,1)S(1)}, u32[]{:S(2)}, u32[]{:S(2)}) collective-permute-start(bf16[12,1152]{1,0:T(8,128)(2,1)S(1)} %collective-permute-done.1), channel_id=1, source_target_pairs={{448,0},{0,64},{64,128},{128,192},{192,256},{256,320},{320,384},{3... | collective-permute-start | bytes 82952 | tf_op jit(solution)/shard_map/ppermute | solution.py:12
  28.9 8.3 %collective-permute-start.5 = (bf16[12,1152]{1,0:T(8,128)(2,1)S(1)}, bf16[12,1152]{1,0:T(8,128)(2,1)S(1)}, u32[]{:S(2)}, u32[]{:S(2)}) collective-permute-start(bf16[12,1152]{1,0:T(8,128)(2,1)S(1)} %collective-permute-done.3), channel_id=1, source_target_pairs={{448,0},{0,64},{64,128},{128,192},{192,256},{256,320},{320,384},{3... | collective-permute-start | bytes 82952 | tf_op jit(solution)/shard_map/ppermute | solution.py:12
  37.2 8.7 %collective-permute-start.7 = (bf16[12,1152]{1,0:T(8,128)(2,1)S(1)}, bf16[12,1152]{1,0:T(8,128)(2,1)S(1)}, u32[]{:S(2)}, u32[]{:S(2)}) collective-permute-start(bf16[12,1152]{1,0:T(8,128)(2,1)S(1)} %collective-permute-done.5), channel_id=1, source_target_pairs={{448,0},{0,64},{64,128},{128,192},{192,256},{256,320},{320,384},{3... | collective-permute-start | bytes 82952 | tf_op jit(solution)/shard_map/ppermute | solution.py:12
  45.9 8.5 %collective-permute-start.9 = (bf16[12,1152]{1,0:T(8,128)(2,1)S(1)}, bf16[12,1152]{1,0:T(8,128)(2,1)S(1)}, u32[]{:S(2)}, u32[]{:S(2)}) collective-permute-start(bf16[12,1152]{1,0:T(8,128)(2,1)S(1)} %collective-permute-done.7), channel_id=1, source_target_pairs={{448,0},{0,64},{64,128},{128,192},{192,256},{256,320},{320,384},{3... | collective-permute-start | bytes 82952 | tf_op jit(solution)/shard_map/ppermute | solution.py:12
  54.4 8.3 %collective-permute-start.11 = (bf16[12,1152]{1,0:T(8,128)(2,1)S(1)}, bf16[12,1152]{1,0:T(8,128)(2,1)S(1)}, u32[]{:S(2)}, u32[]{:S(2)}) collective-permute-start(bf16[12,1152]{1,0:T(8,128)(2,1)S(1)} %collective-permute-done.9), channel_id=1, source_target_pairs={{448,0},{0,64},{64,128},{128,192},{192,256},{256,320},{320,384},{3... | collective-permute-start | bytes 82952 | tf_op jit(solution)/shard_map/ppermute | solution.py:12
  62.7 88.8 %collective-permute-start.13 = (bf16[12,1152]{1,0:T(8,128)(2,1)S(1)}, bf16[12,1152]{1,0:T(8,128)(2,1)S(1)}, u32[]{:S(2)}, u32[]{:S(2)}) collective-permute-start(bf16[12,1152]{1,0:T(8,128)(2,1)S(1)} %collective-permute-done.11), channel_id=1, source_target_pairs={{448,0},{0,64},{64,128},{128,192},{192,256},{256,320},{320,384},{3... | collective-permute-start | bytes 82952 | tf_op jit(solution)/shard_map/ppermute | solution.py:12
  143.6 144.5 %collective-permute-start = (f32[12,1152]{1,0:T(8,128)S(1)}, f32[12,1152]{1,0:T(8,128)S(1)}, u32[]{:S(2)}, u32[]{:S(2)}) collective-permute-start(f32[12,1152]{1,0:T(8,128)S(1)} %convolution_multiply_fusion.7), channel_id=1, source_target_pairs={{448,0},{0,64},{64,128},{128,192},{192,256},{256,320},{320,384},{3... | collective-permute-start | bytes 165896 | tf_op jit(solution)/shard_map/ppermute | solution.py:12
  288.4 8.7 %collective-permute-start.2 = (f32[12,1152]{1,0:T(8,128)S(1)}, f32[12,1152]{1,0:T(8,128)S(1)}, u32[]{:S(2)}, u32[]{:S(2)}) collective-permute-start(f32[12,1152]{1,0:T(8,128)S(1)} %fusion.7), channel_id=1, source_target_pairs={{448,0},{0,64},{64,128},{128,192},{192,256},{256,320},{320,384},{3... | collective-permute-start | bytes 165896 | tf_op jit(solution)/shard_map/ppermute | solution.py:12
  297.1 18.4 %collective-permute-start.4 = (f32[12,1152]{1,0:T(8,128)S(1)}, f32[12,1152]{1,0:T(8,128)S(1)}, u32[]{:S(2)}, u32[]{:S(2)}) collective-permute-start(f32[12,1152]{1,0:T(8,128)S(1)} %add.199), channel_id=1, source_target_pairs={{448,0},{0,64},{64,128},{128,192},{192,256},{256,320},{320,384},{3... | collective-permute-start | bytes 165896 | tf_op jit(solution)/shard_map/ppermute | solution.py:12
  300.0 27.1 %collective-permute-start.29 = (f32[16,1152]{1,0:T(8,128)S(1)}, f32[16,1152]{1,0:T(8,128)S(1)}, u32[]{:S(2)}, u32[]{:S(2)}) collective-permute-start(f32[16,1152]{1,0:T(8,128)S(1)} %fusion), channel_id=1, source_target_pairs={{0,15},{1,16},{2,17},{3,18},{4,19},{5,20},{6,21},{7,22},{8,23},{9,... | collective-permute-start | bytes 221192
  308.8 28.1 %collective-permute-start.28 = (f32[16,1152]{1,0:T(8,128)S(1)}, f32[16,1152]{1,0:T(8,128)S(1)}, u32[]{:S(2)}, u32[]{:S(2)}) collective-permute-start(f32[16,1152]{1,0:T(8,128)S(1)} %fusion), channel_id=1, source_target_pairs={{0,14},{1,15},{2,16},{3,17},{4,18},{5,19},{6,20},{7,21},{8,22},{9,... | collective-permute-start | bytes 221192
  310.1 15.8 %collective-permute-start.30 = (f32[12,1152]{1,0:T(8,128)S(1)}, f32[12,1152]{1,0:T(8,128)S(1)}, u32[]{:S(2)}, u32[]{:S(2)}) collective-permute-start(f32[12,1152]{1,0:T(8,128)S(1)} %slice), channel_id=1, source_target_pairs={{0,16},{1,17},{2,18},{3,19},{4,20},{5,21},{6,22},{7,23},{8,24},{9,... | collective-permute-start | bytes 165896
  315.5 9.0 %collective-permute-start.6 = (f32[12,1152]{1,0:T(8,128)S(1)}, f32[12,1152]{1,0:T(8,128)S(1)}, u32[]{:S(2)}, u32[]{:S(2)}) collective-permute-start(f32[12,1152]{1,0:T(8,128)S(1)} %add.204), channel_id=1, source_target_pairs={{448,0},{0,64},{64,128},{128,192},{192,256},{256,320},{320,384},{3... | collective-permute-start | bytes 165896 | tf_op jit(solution)/shard_map/ppermute | solution.py:12
  320.7 19.3 %collective-permute-start.27 = (f32[16,1152]{1,0:T(8,128)S(1)}, f32[16,1152]{1,0:T(8,128)S(1)}, u32[]{:S(2)}, u32[]{:S(2)}) collective-permute-start(f32[16,1152]{1,0:T(8,128)S(1)} %fusion), channel_id=1, source_target_pairs={{0,13},{1,14},{2,15},{3,16},{4,17},{5,18},{6,19},{7,20},{8,21},{9,... | collective-permute-start | bytes 221192
  324.5 17.7 %collective-permute-start.26 = (f32[16,1152]{1,0:T(8,128)S(1)}, f32[16,1152]{1,0:T(8,128)S(1)}, u32[]{:S(2)}, u32[]{:S(2)}) collective-permute-start(f32[16,1152]{1,0:T(8,128)S(1)} %fusion), channel_id=1, source_target_pairs={{0,12},{1,13},{2,14},{3,15},{4,16},{5,17},{6,18},{7,19},{8,20},{9,... | collective-permute-start | bytes 221192
  325.8 17.7 %collective-permute-start.25 = (f32[16,1152]{1,0:T(8,128)S(1)}, f32[16,1152]{1,0:T(8,128)S(1)}, u32[]{:S(2)}, u32[]{:S(2)}) collective-permute-start(f32[16,1152]{1,0:T(8,128)S(1)} %fusion), channel_id=1, source_target_pairs={{0,11},{1,12},{2,13},{3,14},{4,15},{5,16},{6,17},{7,18},{8,19},{9,... | collective-permute-start | bytes 221192
  327.1 25.2 %collective-permute-start.24 = (f32[16,1152]{1,0:T(8,128)S(1)}, f32[16,1152]{1,0:T(8,128)S(1)}, u32[]{:S(2)}, u32[]{:S(2)}) collective-permute-start(f32[16,1152]{1,0:T(8,128)S(1)} %fusion), channel_id=1, source_target_pairs={{0,10},{1,11},{2,12},{3,13},{4,14},{5,15},{6,16},{7,17},{8,18},{9,... | collective-permute-start | bytes 221192
  336.8 18.9 %collective-permute-start.8 = (f32[12,1152]{1,0:T(8,128)S(1)}, f32[12,1152]{1,0:T(8,128)S(1)}, u32[]{:S(2)}, u32[]{:S(2)}) collective-permute-start(f32[12,1152]{1,0:T(8,128)S(1)} %add.209), channel_id=1, source_target_pairs={{448,0},{0,64},{64,128},{128,192},{192,256},{256,320},{320,384},{3... | collective-permute-start | bytes 165896 | tf_op jit(solution)/shard_map/ppermute | solution.py:12
  340.0 19.0 %collective-permute-start.23 = (f32[16,1152]{1,0:T(8,128)S(1)}, f32[16,1152]{1,0:T(8,128)S(1)}, u32[]{:S(2)}, u32[]{:S(2)}) collective-permute-start(f32[16,1152]{1,0:T(8,128)S(1)} %fusion), channel_id=1, source_target_pairs={{0,9},{1,10},{2,11},{3,12},{4,13},{5,14},{6,15},{7,16},{8,17},{9,1... | collective-permute-start | bytes 221192
  342.2 20.1 %collective-permute-start.22 = (f32[16,1152]{1,0:T(8,128)S(1)}, f32[16,1152]{1,0:T(8,128)S(1)}, u32[]{:S(2)}, u32[]{:S(2)}) collective-permute-start(f32[16,1152]{1,0:T(8,128)S(1)} %fusion), channel_id=1, source_target_pairs={{0,8},{1,9},{2,10},{3,11},{4,12},{5,13},{6,14},{7,15},{8,16},{9,17... | collective-permute-start | bytes 221192
  343.6 20.1 %collective-permute-start.21 = (f32[16,1152]{1,0:T(8,128)S(1)}, f32[16,1152]{1,0:T(8,128)S(1)}, u32[]{:S(2)}, u32[]{:S(2)}) collective-permute-start(f32[16,1152]{1,0:T(8,128)S(1)} %fusion), channel_id=1, source_target_pairs={{0,7},{1,8},{2,9},{3,10},{4,11},{5,12},{6,13},{7,14},{8,15},{9,16}... | collective-permute-start | bytes 221192
  352.4 14.4 %collective-permute-start.20 = (f32[16,1152]{1,0:T(8,128)S(1)}, f32[16,1152]{1,0:T(8,128)S(1)}, u32[]{:S(2)}, u32[]{:S(2)}) collective-permute-start(f32[16,1152]{1,0:T(8,128)S(1)} %fusion), channel_id=1, source_target_pairs={{0,6},{1,7},{2,8},{3,9},{4,10},{5,11},{6,12},{7,13},{8,14},{9,15},... | collective-permute-start | bytes 221192
  355.7 14.2 %collective-permute-start.19 = (f32[16,1152]{1,0:T(8,128)S(1)}, f32[16,1152]{1,0:T(8,128)S(1)}, u32[]{:S(2)}, u32[]{:S(2)}) collective-permute-start(f32[16,1152]{1,0:T(8,128)S(1)} %fusion), channel_id=1, source_target_pairs={{0,5},{1,6},{2,7},{3,8},{4,9},{5,10},{6,11},{7,12},{8,13},{9,14},{... | collective-permute-start | bytes 221192
  359.0 13.2 %collective-permute-start.18 = (f32[16,1152]{1,0:T(8,128)S(1)}, f32[16,1152]{1,0:T(8,128)S(1)}, u32[]{:S(2)}, u32[]{:S(2)}) collective-permute-start(f32[16,1152]{1,0:T(8,128)S(1)} %fusion), channel_id=1, source_target_pairs={{0,4},{1,5},{2,6},{3,7},{4,8},{5,9},{6,10},{7,11},{8,12},{9,13},{1... | collective-permute-start | bytes 221192
  362.4 9.8 %collective-permute-start.17 = (f32[16,1152]{1,0:T(8,128)S(1)}, f32[16,1152]{1,0:T(8,128)S(1)}, u32[]{:S(2)}, u32[]{:S(2)}) collective-permute-start(f32[16,1152]{1,0:T(8,128)S(1)} %fusion), channel_id=1, source_target_pairs={{0,3},{1,4},{2,5},{3,6},{4,7},{5,8},{6,9},{7,10},{8,11},{9,12},{10... | collective-permute-start | bytes 221192
  363.7 8.5 %collective-permute-start.16 = (f32[16,1152]{1,0:T(8,128)S(1)}, f32[16,1152]{1,0:T(8,128)S(1)}, u32[]{:S(2)}, u32[]{:S(2)}) collective-permute-start(f32[16,1152]{1,0:T(8,128)S(1)} %fusion), channel_id=1, source_target_pairs={{0,2},{1,3},{2,4},{3,5},{4,6},{5,7},{6,8},{7,9},{8,10},{9,11},{10,... | collective-permute-start | bytes 221192
  366.8 5.4 %collective-permute-start.15 = (f32[16,1152]{1,0:T(8,128)S(1)}, f32[16,1152]{1,0:T(8,128)S(1)}, u32[]{:S(2)}, u32[]{:S(2)}) collective-permute-start(f32[16,1152]{1,0:T(8,128)S(1)} %fusion), channel_id=1, source_target_pairs={{0,1},{1,2},{2,3},{3,4},{4,5},{5,6},{6,7},{7,8},{8,9},{9,10},{10,1... | collective-permute-start | bytes 221192
  369.9 9.7 %collective-permute-start.10 = (f32[12,1152]{1,0:T(8,128)S(1)}, f32[12,1152]{1,0:T(8,128)S(1)}, u32[]{:S(2)}, u32[]{:S(2)}) collective-permute-start(f32[12,1152]{1,0:T(8,128)S(1)} %add.214), channel_id=1, source_target_pairs={{448,0},{0,64},{64,128},{128,192},{192,256},{256,320},{320,384},{3... | collective-permute-start | bytes 165896 | tf_op jit(solution)/shard_map/ppermute | solution.py:12
  379.6 8.7 %collective-permute-start.12 = (f32[12,1152]{1,0:T(8,128)S(1)}, f32[12,1152]{1,0:T(8,128)S(1)}, u32[]{:S(2)}, u32[]{:S(2)}) collective-permute-start(f32[12,1152]{1,0:T(8,128)S(1)} %add.219), channel_id=1, source_target_pairs={{448,0},{0,64},{64,128},{128,192},{192,256},{256,320},{320,384},{3... | collective-permute-start | bytes 165896 | tf_op jit(solution)/shard_map/ppermute | solution.py:12
  388.3 8.7 %collective-permute-start.14 = (f32[12,1152]{1,0:T(8,128)S(1)}, f32[12,1152]{1,0:T(8,128)S(1)}, u32[]{:S(2)}, u32[]{:S(2)}) collective-permute-start(f32[12,1152]{1,0:T(8,128)S(1)} %add.224), channel_id=1, source_target_pairs={{448,0},{0,64},{64,128},{128,192},{192,256},{256,320},{320,384},{3... | collective-permute-start | bytes 165896 | tf_op jit(solution)/shard_map/ppermute | solution.py:12
  (2 other events, 91.6 us)
Sparse Core Ops, SparseCore 0:
  10.7 128.6 all-gather.2
where the time goes:
time: 407 us; the launch traced here: 405 us
  waiting for transfers between devices  131 us (32%)
  blocking collectives  129 us (32%)
  starting transfers between devices  101 us (25%)
  between operations  16.7 us (4%)
  matrix products  15.5 us (4%)
  local copies, waits for them, and re-layouts  6.09 us (1%)
  other arithmetic  6.01 us (1%)
    unnamed x1, blocking collectives  129 us
    all_gather x1, waiting for transfers between devices, shards(): text_block = lax.all_gather(text_half, 'grp', axis=0, tiled=True)  74.7 us
    unnamed x16, starting transfers between devices  58.3 us
    ppermute x15, waiting for transfers between devices, from_behind(): return lax.ppermute(block, axis, route)  56.4 us
    ppermute x15, starting transfers between devices, from_behind(): return lax.ppermute(block, axis, route)  42.2 us
  transfers between devices with their start and end apart: 32, of which 12 were waited for; matrix products, arithmetic and copies ran while one was open for 38% of the time, Pallas kernels for 0%

commit v1 on v0

v1 whole, which is shorter than its diff:
```python
import jax
import jax.numpy as jnp
from jax import lax
from jax.experimental import pallas as pl
from jax.experimental.pallas import tpu as pltpu
from jax.sharding import PartitionSpec as P

EPS = 1e-06
MESH = pl.DeviceIdType.MESH
ROWS = 16
USED = 12
LANES = 128
MAIN = 7 * LANES
REST = 2 * LANES
F32 = jnp.float32
BF16 = jnp.bfloat16
AROUND = (3, 2, 1)


class Place:
    def __init__(self):
        blk, grp = lax.axis_index("blk"), lax.axis_index("grp")
        self.y = blk // 2
        self.z = grp // 4
        self.x = (blk % 2) * 2 + (grp // 2) % 2
        self.core = grp % 2

    def at(self, x, y, z, core):
        return (y * 2 + x // 2, z * 4 + (x % 2) * 2 + core)

    def other_core(self):
        return self.at(self.x, self.y, self.z, 1 - self.core)

    def text_plane(self, k):
        x = self.x + (k % 2) * (1 - 2 * (self.x % 2))
        y = self.y + (k // 2) * (1 - 2 * (self.y % 2))
        return self.at(x, y, self.z, self.core)

    def image_plane(self, k):
        x = (self.x + (k % 2) * (2 * (self.x % 2) + 3)) % 4
        y = (self.y + (k // 2) * (2 * (self.y % 2) + 3)) % 4
        return self.at(x, y, self.z, self.core)

    def text_z(self, k):
        z = self.z + (k % 2) * (1 - 2 * (self.z % 2)) + (k // 2) * (4 - 8 * ((self.z // 4) % 2))
        return self.at(self.x, self.y, z, self.core)

    def image_z(self, k):
        z = self.z + (k % 2) * (2 - 4 * ((self.z // 2) % 2)) + (k // 2) * (8 * ((self.z // 4) % 2) + 12)
        return self.at(self.x, self.y, z % 16, self.core)


def pieces_up(rest):
    low, high = rest[:, 0:8], rest[:, 8:16]
    low_up, high_up = pltpu.roll(low, 4, 1), pltpu.roll(high, 4, 1)
    parts = []
    for c in (slice(0, LANES), slice(LANES, REST)):
        parts += [low_up[:, :, c], low[:, :, c], high_up[:, :, c]]
    return jnp.concatenate(parts + [jnp.zeros_like(parts[0])], axis=2)


def pack(main, rest):
    pieces = pieces_up(rest)
    lower = lax.broadcasted_iota(jnp.int32, pieces.shape, 1) >= 4
    return jnp.concatenate([main[:, 0:8], jnp.where(lower, pieces, main[:, 8:16])], axis=1)


def unpack_rest(packed):
    under = packed[:, 8:16]
    up = pltpu.roll(under, 4, 1)
    lower = lax.broadcasted_iota(jnp.int32, under[:, :, 0:LANES].shape, 1) >= 4
    lows, highs = [], []
    for c in (0, 3):
        first, second, third = (slice((c + i) * LANES, (c + i + 1) * LANES) for i in range(3))
        lows.append(jnp.where(lower, under[:, :, second], up[:, :, first]))
        highs.append(jnp.where(lower, 0.0, up[:, :, third]))
    return jnp.concatenate(
        [jnp.concatenate(lows, axis=2), jnp.concatenate(highs, axis=2)], axis=1
    )


def dot(a, b, dims):
    return lax.dot_general(a, b, (dims, ((), ())), preferred_element_type=F32)


def kernel(
    scale_ref,
    bias_ref,
    image_hbm,
    text_hbm,
    image_out,
    text_out,
    raw,
    units,
    grads,
    texts,
    images,
    texts_rest,
    images_rest,
    image_coefs,
    text_coefs,
    text_terms,
    image_terms,
    text_plane_out,
    text_plane_in,
    image_plane_out,
    image_plane_in,
    text_z_out,
    text_z_in,
    image_z_out,
    image_z_in,
    load_sems,
    send_sems,
    text_z_recv,
    text_plane_recv,
    image_z_recv,
    image_plane_recv,
    text_core_recv,
    image_core_recv,
    text_back_recv,
    image_back_recv,
    last_recv,
):
    loads = [
        pltpu.make_async_copy(image_hbm, raw.at[0], load_sems.at[0]),
        pltpu.make_async_copy(text_hbm, raw.at[1], load_sems.at[1]),
    ]
    for one in loads:
        one.start()
    place = Place()
    partner = place.other_core()
    text_plane, image_plane, image_z, text_z = (
        {k: way(k) for k in AROUND} for way in (place.text_plane, place.image_plane, place.image_z, place.text_z)
    )
    barrier = pltpu.get_barrier_semaphore()
    for k in AROUND:
        for device in (text_z[k], image_z[k], text_plane[k], image_plane[k]):
            pl.semaphore_signal(barrier, inc=1, device_id=device, device_id_type=MESH)
    pl.semaphore_signal(barrier, inc=1, device_id=partner, device_id_type=MESH)
    units[...] = jnp.zeros_like(units)
    for one in loads:
        one.wait()
    values = raw[...].astype(F32)
    recip = lax.rsqrt(jnp.sum(values * values, axis=2, keepdims=True) + EPS)
    units[:, 0:USED] = values * recip
    own = units[...]
    own_rest = own[:, :, MAIN:]
    own_packed = pack(own[:, :, :MAIN], own_rest).astype(BF16)
    images[0, 0, 0] = own_packed[0]
    texts[0, 0, 0] = own_packed[1]
    pl.semaphore_wait(barrier, 13)

    def remote(src, dst, send, recv, device):
        return pltpu.make_async_remote_copy(
            src_ref=src,
            dst_ref=dst,
            send_sem=send_sems.at[send],
            recv_sem=recv,
            device_id=device,
            device_id_type=MESH,
        )

    def arrived(ref, recv):
        remote(ref, ref, 0, recv, partner).wait_recv()

    def left(ref, send):
        remote(ref, ref, send, text_core_recv.at[0], partner).wait_send()

    def spread(blocks, plane, send, recv, dz):
        for k in AROUND:
            remote(blocks.at[0, dz, 0], blocks.at[0, dz, k], send, recv.at[dz], plane[k]).start()

    def complete(blocks, rests, plane_recv, send, core_recv, dz):
        arrived(blocks.at[0, dz, pl.ds(1, 3)], plane_recv.at[dz])
        remote(blocks.at[0, dz], blocks.at[1, dz], send, core_recv.at[dz], partner).start()
        rests[0, dz] = unpack_rest(blocks[0, dz].astype(F32)).astype(BF16)

    def partner_complete(blocks, rests, core_recv, dz):
        arrived(blocks.at[1, dz], core_recv.at[dz])
        rests[1, dz] = unpack_rest(blocks[1, dz].astype(F32)).astype(BF16)

    for k in AROUND:
        remote(texts.at[0, 0, 0], texts.at[0, k, 0], 0, text_z_recv.at[k], text_z[k]).start()
    for k in AROUND:
        remote(images.at[0, 0, 0], images.at[0, k, 0], 2, image_z_recv.at[k], image_z[k]).start()
    spread(texts, text_plane, 1, text_plane_recv, 0)
    spread(images, image_plane, 3, image_plane_recv, 0)
    for dz in (1, 2, 3):
        arrived(texts.at[0, dz, 0], text_z_recv.at[dz])
        spread(texts, text_plane, 1, text_plane_recv, dz)
        arrived(images.at[0, dz, 0], image_z_recv.at[dz])
        spread(images, image_plane, 3, image_plane_recv, dz)
    for dz in range(4):
        complete(texts, texts_rest, text_plane_recv, 4, text_core_recv, dz)
        complete(images, images_rest, image_plane_recv, 5, image_core_recv, dz)

    scale, bias = scale_ref[()], bias_ref[()]
    half = 16 * ROWS
    across = ((1,), (1,))

    def flat(ref, lane):
        return ref[lane].reshape(half, ref.shape[-1])

    def coefficients(rows, cols, col_lane):
        logits = dot(flat(rows[0], 0), flat(cols[0], col_lane), across)
        logits = logits + dot(flat(rows[1], 0), flat(cols[1], col_lane), across)
        logits = scale * logits + bias
        row = lax.broadcasted_iota(jnp.int32, logits.shape, 0)
        col = lax.broadcasted_iota(jnp.int32, logits.shape, 1)
        held = jnp.logical_and(row % ROWS < USED, col % ROWS < USED)
        return logits, held, jnp.where(held, jax.nn.sigmoid(logits), 0.0).astype(BF16)

    def own_coefficients(ref, rows, cols):
        logits, held, ref[:, own] = coefficients(rows, cols, 0)
        corner = (slice(0, ROWS), slice(0, LANES))
        logits, held = logits[corner], held[corner]
        row = lax.broadcasted_iota(jnp.int32, (ROWS, LANES), 0)
        col = lax.broadcasted_iota(jnp.int32, (ROWS, LANES), 1)
        pairs = jnp.where(row == col, -jax.nn.sigmoid(-logits), jax.nn.sigmoid(logits))
        ref[corner] = jnp.where(held, pairs, 0.0).astype(BF16)

    own, other = slice(0, half), slice(half, 2 * half)
    all_images, all_texts = (images, images_rest), (texts, texts_rest)
    own_coefficients(image_coefs, all_images, all_texts)
    own_coefficients(text_coefs, all_texts, all_images)

    def returns(coefs, cols, dz, terms, out, into, send, recv, plane):
        factor = coefs[4 * ROWS * dz : 4 * ROWS * (dz + 1), :]
        main, rest = (
            dot(factor, ref[...].reshape(2 * half, ref.shape[-1]), ((1,), (0,))).reshape(4, ROWS, ref.shape[-1])
            for ref in cols
        )
        packed = pack(main, rest)
        terms[dz] = packed[0]
        out[dz] = packed[1:4].astype(BF16)
        for k in AROUND:
            remote(out.at[dz, k - 1], into.at[dz, k - 1], send, recv.at[dz], plane[k]).start()

    def image_returns(dz):
        returns(
            image_coefs, all_texts, dz, image_terms, image_plane_out, image_plane_in, 6, image_back_recv, image_plane
        )

    def text_returns(dz):
        returns(text_coefs, all_images, dz, text_terms, text_plane_out, text_plane_in, 7, text_back_recv, text_plane)

    for dz in range(4):
        partner_complete(texts, texts_rest, text_core_recv, dz)
    image_coefs[:, other] = coefficients(all_images, all_texts, 1)[2]
    image_returns(3)
    for dz in range(4):
        partner_complete(images, images_rest, image_core_recv, dz)
    text_coefs[:, other] = coefficients(all_texts, all_images, 1)[2]
    text_returns(3)
    for dz in (2, 1):
        image_returns(dz)
        text_returns(dz)

    def summed(dz, terms, into, recv):
        arrived(into.at[dz], recv.at[dz])
        return terms[dz] + jnp.sum(into[dz].astype(F32), axis=0)

    def image_sum(dz):
        return summed(dz, image_terms, image_plane_in, image_back_recv)

    def text_sum(dz):
        return summed(dz, text_terms, text_plane_in, text_back_recv)

    def z_returns(k):
        image_z_out[k - 1] = image_sum(k).astype(BF16)
        remote(image_z_out.at[k - 1], image_z_in.at[k - 1], 8, last_recv.at[0], image_z[k]).start()
        text_z_out[k - 1] = text_sum(k).astype(BF16)
        remote(text_z_out.at[k - 1], text_z_in.at[k - 1], 9, last_recv.at[1], text_z[k]).start()

    z_returns(3)
    image_returns(0)
    text_returns(0)
    z_returns(2)
    z_returns(1)
    for blocks, first in ((texts, 0), (images, 2)):
        left(blocks.at[0, 0, pl.ds(1, 3)], first)
        left(blocks.at[0, pl.ds(1, 3)], first + 1)
        left(blocks.at[0], first // 2 + 4)
    image_total = image_sum(0)
    text_total = text_sum(0)
    left(image_plane_out, 6)
    left(text_plane_out, 7)

    def finish(i, out, total, ref):
        arrived(ref, last_recv.at[i])
        total = scale * (total + jnp.sum(ref[...].astype(F32), axis=0))
        grads[i, :, :MAIN] = total
        grads[i, :, MAIN:] = unpack_rest(total[None])[0]
        grad, unit = grads[i, 0:USED], units[i, 0:USED]
        out[...] = recip[i] * (grad - unit * jnp.sum(unit * grad, axis=1, keepdims=True))

    finish(0, image_out, image_total, image_z_in)
    finish(1, text_out, text_total, text_z_in)
    left(image_z_out, 8)
    left(text_z_out, 9)


def shards(image_embed, text_embed, logit_scale, logit_bias):
    rows, width = image_embed.shape
    vmem = pl.BlockSpec(memory_space=pltpu.VMEM)
    hbm = pl.BlockSpec(memory_space=pltpu.HBM)
    out = jax.ShapeDtypeStruct((rows, width), F32)

    def half(*lead, columns=MAIN):
        return pltpu.VMEM((*lead, ROWS, columns), BF16)

    def full(*lead, columns=MAIN):
        return pltpu.VMEM((*lead, ROWS, columns), F32)

    def dma(*shape):
        return pltpu.SemaphoreType.DMA(shape)

    return pl.pallas_call(
        kernel,
        out_shape=(out, out),
        in_specs=[pl.BlockSpec(memory_space=pltpu.SMEM)] * 2 + [hbm, hbm],
        out_specs=(vmem, vmem),
        scratch_shapes=[
            pltpu.VMEM((2, rows, width), BF16),
            full(2, columns=width),
            full(2, columns=width),
            half(2, 4, 4),
            half(2, 4, 4),
            half(2, 4, 4, columns=REST),
            half(2, 4, 4, columns=REST),
            pltpu.VMEM((16 * ROWS, 32 * ROWS), BF16),
            pltpu.VMEM((16 * ROWS, 32 * ROWS), BF16),
            full(4),
            full(4),
            half(4, 3),
            half(4, 3),
            half(4, 3),
            half(4, 3),
            half(3),
            half(3),
            half(3),
            half(3),
            dma(2),
            dma(10),
            dma(4),
            dma(4),
            dma(4),
            dma(4),
            dma(4),
            dma(4),
            dma(4),
            dma(4),
            dma(2),
        ],
        compiler_params=pltpu.CompilerParams(
            collective_id=0, has_side_effects=True, vmem_limit_bytes=40 * 1024 * 1024
        ),
    )(
        logit_scale,
        logit_bias,
        pltpu.with_memory_space_constraint(image_embed, pltpu.HBM),
        pltpu.with_memory_space_constraint(text_embed, pltpu.HBM),
    )


def solution(mesh):
    return jax.shard_map(
        shards,
        mesh=mesh,
        in_specs=(P(("blk", "grp"), None), P(("blk", "grp"), None), P(), P()),
        out_specs=(P(("blk", "grp"), None), P(("blk", "grp"), None)),
        check_vma=False,
    )
```

time: 407 us -> 47.4 us (0.12)
  waiting for transfers between devices: 131 us -> 0 us
  blocking collectives: 129 us -> 0 us
  starting transfers between devices: 101 us -> 0 us
  Pallas kernels: 0 us -> 44 us
  matrix products: 15.5 us -> 0 us
  between operations: 16.7 us -> 1.93 us
  other arithmetic: 6.01 us -> 0 us
  local copies, waits for them, and re-layouts: 6.09 us -> 1.27 us
    unnamed x1 -> x0, blocking collectives: 129 us -> none
    all_gather x1 -> x0, waiting for transfers between devices: 74.7 us -> none  [shards(): text_block = lax.all_gather(text_half, 'grp', axis=0, tiled=True)]
    unnamed x16 -> x0, starting transfers between devices: 58.3 us -> none
    ppermute x15 -> x0, waiting for transfers between devices: 56.4 us -> none  [from_behind(): return lax.ppermute(block, axis, route)]
    pallas_call x0 -> x1, Pallas kernels: none -> 44 us  [shards(): pl.pallas_call(kernel, out_shape=(out, out), in_specs=[pl.BlockSpec(memor...]
    ppermute x15 -> x0, starting transfers between devices: 42.2 us -> none  [from_behind(): return lax.ppermute(block, axis, route)]
    dot_general x24 -> x0, matrix products: 15.5 us -> none  [the longest x8 7.85 us: record(): lax.dot_general(coef, visit, (((0,), (0,)), ((), ())), preferred_element_...]
    unnamed x8 -> x2, local copies, waits for them, and re-layouts: 6.09 us -> 1.27 us
  transfers between devices with their start and end apart: 32 -> 0, of which waited for: 12 -> 0; matrix products, arithmetic and copies ran while one was open for 38% -> 0% of each run, Pallas kernels for 0% -> 0%
where the time goes in v1:
time: 47.4 us; the launch traced here: 47.2 us
  Pallas kernels  44 us (93%)
  between operations  1.93 us (4%)
  local copies, waits for them, and re-layouts  1.27 us (3%)
    pallas_call x1, Pallas kernels, shards(): pl.pallas_call(kernel, out_shape=(out, out), in_specs=[pl.BlockSpec(memor...  44 us
    unnamed x2, local copies, waits for them, and re-layouts  1.27 us

profile of v1, /device:TPU:1, one launch (start us, length us, event | category | flops | bytes accessed | tf_op | source)
XLA Modules:
  0.0 47.2 jit_solution(17204981547066905300)
XLA Ops:
  1.9 44.0 %shard_map.59 = (f32[12,1152]{1,0:T(8,128)S(1)}, f32[12,1152]{1,0:T(8,128)S(1)}) custom-call(f32[]{:T(128)S(6)} %copy.8.scale_ref, f32[]{:T(128)S(6)} %copy.9.bias_ref, bf16[12,1152]{1,0:T(8,128)(2,1)} %image_hbm.1, bf16[12,1152]{1,0:T(8,128)(2,1)} %text_hbm.1), custom_call_target="tpu_custom_call" | custom-call | tf_op jit(solution)/shard_map/pallas_call | solution.py:318
  45.9 0.6 %copy.10 = f32[12,1152]{1,0:T(8,128)} copy(f32[12,1152]{1,0:T(8,128)S(1)} %get-tuple-element.4) | data formatting | bytes 110592
  46.6 0.6 %copy.11 = f32[12,1152]{1,0:T(8,128)} copy(f32[12,1152]{1,0:T(8,128)S(1)} %get-tuple-element.5) | data formatting | bytes 110592

commit v2 on v1

--- a/solution.py
+++ b/solution.py
@@ -88,8 +88,7 @@
     bias_ref,
     image_hbm,
     text_hbm,
-    image_out,
-    text_out,
+    both_out,
     raw,
     units,
     grads,
@@ -170,10 +169,13 @@
         for k in AROUND:
             remote(blocks.at[0, dz, 0], blocks.at[0, dz, k], send, recv.at[dz], plane[k]).start()
 
-    def complete(blocks, rests, plane_recv, send, core_recv, dz):
+    def to_partner(blocks, plane_recv, send, core_recv, dz):
         arrived(blocks.at[0, dz, pl.ds(1, 3)], plane_recv.at[dz])
         remote(blocks.at[0, dz], blocks.at[1, dz], send, core_recv.at[dz], partner).start()
-        rests[0, dz] = unpack_rest(blocks[0, dz].astype(F32)).astype(BF16)
+
+    def unpack_set(lane, dz):
+        for blocks, rests in ((texts, texts_rest), (images, images_rest)):
+            rests[lane, dz] = unpack_rest(blocks[lane, dz].astype(F32)).astype(BF16)
 
     def partner_complete(blocks, rests, core_recv, dz):
         arrived(blocks.at[1, dz], core_recv.at[dz])
@@ -185,14 +187,23 @@
         remote(images.at[0, 0, 0], images.at[0, k, 0], 2, image_z_recv.at[k], image_z[k]).start()
     spread(texts, text_plane, 1, text_plane_recv, 0)
     spread(images, image_plane, 3, image_plane_recv, 0)
-    for dz in (1, 2, 3):
+    def forward(dz):
         arrived(texts.at[0, dz, 0], text_z_recv.at[dz])
         spread(texts, text_plane, 1, text_plane_recv, dz)
         arrived(images.at[0, dz, 0], image_z_recv.at[dz])
         spread(images, image_plane, 3, image_plane_recv, dz)
-    for dz in range(4):
-        complete(texts, texts_rest, text_plane_recv, 4, text_core_recv, dz)
-        complete(images, images_rest, image_plane_recv, 5, image_core_recv, dz)
+
+    def across_cores(dz):
+        to_partner(texts, text_plane_recv, 4, text_core_recv, dz)
+        to_partner(images, image_plane_recv, 5, image_core_recv, dz)
+
+    for dz in (1, 2, 3):
+        forward(dz)
+    across_cores(0)
+    for dz in (1, 2, 3):
+        across_cores(dz)
+        unpack_set(0, dz - 1)
+    unpack_set(0, 3)
 
     scale, bias = scale_ref[()], bias_ref[()]
     half = 16 * ROWS
@@ -266,17 +277,21 @@
     def text_sum(dz):
         return summed(dz, text_terms, text_plane_in, text_back_recv)
 
-    def z_returns(k):
+    def image_z_return(k):
         image_z_out[k - 1] = image_sum(k).astype(BF16)
         remote(image_z_out.at[k - 1], image_z_in.at[k - 1], 8, last_recv.at[0], image_z[k]).start()
+
+    def text_z_return(k):
         text_z_out[k - 1] = text_sum(k).astype(BF16)
         remote(text_z_out.at[k - 1], text_z_in.at[k - 1], 9, last_recv.at[1], text_z[k]).start()
 
-    z_returns(3)
+    image_z_return(3)
     image_returns(0)
+    text_z_return(3)
     text_returns(0)
-    z_returns(2)
-    z_returns(1)
+    for k in (2, 1):
+        image_z_return(k)
+        text_z_return(k)
     for blocks, first in ((texts, 0), (images, 2)):
         left(blocks.at[0, 0, pl.ds(1, 3)], first)
         left(blocks.at[0, pl.ds(1, 3)], first + 1)
@@ -286,16 +301,16 @@
     left(image_plane_out, 6)
     left(text_plane_out, 7)
 
-    def finish(i, out, total, ref):
+    def finish(i, total, ref):
         arrived(ref, last_recv.at[i])
         total = scale * (total + jnp.sum(ref[...].astype(F32), axis=0))
         grads[i, :, :MAIN] = total
         grads[i, :, MAIN:] = unpack_rest(total[None])[0]
         grad, unit = grads[i, 0:USED], units[i, 0:USED]
-        out[...] = recip[i] * (grad - unit * jnp.sum(unit * grad, axis=1, keepdims=True))
-
-    finish(0, image_out, image_total, image_z_in)
-    finish(1, text_out, text_total, text_z_in)
+        both_out[i] = recip[i] * (grad - unit * jnp.sum(unit * grad, axis=1, keepdims=True))
+
+    finish(0, image_total, image_z_in)
+    finish(1, text_total, text_z_in)
     left(image_z_out, 8)
     left(text_z_out, 9)
 
@@ -315,11 +330,11 @@
     def dma(*shape):
         return pltpu.SemaphoreType.DMA(shape)
 
-    return pl.pallas_call(
+    both = pl.pallas_call(
         kernel,
-        out_shape=(out, out),
+        out_shape=jax.ShapeDtypeStruct((2, rows, width), F32),
         in_specs=[pl.BlockSpec(memory_space=pltpu.SMEM)] * 2 + [hbm, hbm],
-        out_specs=(vmem, vmem),
+        out_specs=vmem,
         scratch_shapes=[
             pltpu.VMEM((2, rows, width), BF16),
             full(2, columns=width),
@@ -361,6 +376,7 @@
         pltpu.with_memory_space_constraint(image_embed, pltpu.HBM),
         pltpu.with_memory_space_constraint(text_embed, pltpu.HBM),
     )
+    return both[0], both[1]
 
 
 def solution(mesh):

time: 47.4 us -> 47.6 us (level)
  Pallas kernels: 44 us -> 44.8 us
  local copies, waits for them, and re-layouts: 1.27 us -> 0.66 us
    unnamed x2 -> x0, local copies, waits for them, and re-layouts: 1.27 us -> none
    pallas_call x1, Pallas kernels: 44 us -> 44.8 us  [shards(): pl.pallas_call(kernel, out_shape=jax.ShapeDtypeStruct((2, rows, width), F...]
    squeeze x0 -> x1, local copies, waits for them, and re-layouts: none -> 0.66 us  [shards(): return (both[0], both[1])]
where the time goes in v2:
time: 47.6 us; the launch traced here: 47.4 us
  Pallas kernels  44.8 us (94%)
  between operations  1.93 us (4%)
  local copies, waits for them, and re-layouts  0.66 us (1%)
    pallas_call x1, Pallas kernels, shards(): pl.pallas_call(kernel, out_shape=jax.ShapeDtypeStruct((2, rows, width), F...  44.8 us

profile of v2, /device:TPU:1, one launch (start us, length us, event | category | flops | bytes accessed | tf_op | source)
XLA Modules:
  0.0 47.4 jit_solution(8680011512314572090)
XLA Ops:
  1.9 44.8 %shard_map.59 = f32[2,12,1152]{2,1,0:T(8,128)S(1)} custom-call(f32[]{:T(128)S(6)} %copy.6.scale_ref, f32[]{:T(128)S(6)} %copy.7.bias_ref, bf16[12,1152]{1,0:T(8,128)(2,1)} %image_hbm.1, bf16[12,1152]{1,0:T(8,128)(2,1)} %text_hbm.1), custom_call_target="tpu_custom_call" | custom-call | tf_op jit(solution)/shard_map/pallas_call | solution.py:333
  46.7 0.7 %slice_bitcast_fusion = (f32[12,1152]{1,0:T(8,128)}, f32[12,1152]{1,0:T(8,128)}) fusion(f32[2,12,1152]{2,1,0:T(8,128)S(1)} %shard_map.59), kind=kLoop, calls=%fused_computation | loop fusion | bytes 221184 | tf_op jit(solution)/shard_map/squeeze | solution.py:379

commit v3 on v2

--- a/solution.py
+++ b/solution.py
@@ -173,13 +173,12 @@
         arrived(blocks.at[0, dz, pl.ds(1, 3)], plane_recv.at[dz])
         remote(blocks.at[0, dz], blocks.at[1, dz], send, core_recv.at[dz], partner).start()
 
-    def unpack_set(lane, dz):
-        for blocks, rests in ((texts, texts_rest), (images, images_rest)):
-            rests[lane, dz] = unpack_rest(blocks[lane, dz].astype(F32)).astype(BF16)
+    def unpack_set(blocks, rests, lane, dz):
+        rests[lane, dz] = unpack_rest(blocks[lane, dz].astype(F32)).astype(BF16)
 
     def partner_complete(blocks, rests, core_recv, dz):
         arrived(blocks.at[1, dz], core_recv.at[dz])
-        rests[1, dz] = unpack_rest(blocks[1, dz].astype(F32)).astype(BF16)
+        unpack_set(blocks, rests, 1, dz)
 
     for k in AROUND:
         remote(texts.at[0, 0, 0], texts.at[0, k, 0], 0, text_z_recv.at[k], text_z[k]).start()
@@ -187,23 +186,20 @@
         remote(images.at[0, 0, 0], images.at[0, k, 0], 2, image_z_recv.at[k], image_z[k]).start()
     spread(texts, text_plane, 1, text_plane_recv, 0)
     spread(images, image_plane, 3, image_plane_recv, 0)
-    def forward(dz):
+    for dz in (1, 2, 3):
         arrived(texts.at[0, dz, 0], text_z_recv.at[dz])
         spread(texts, text_plane, 1, text_plane_recv, dz)
+    for dz in (1, 2, 3):
         arrived(images.at[0, dz, 0], image_z_recv.at[dz])
         spread(images, image_plane, 3, image_plane_recv, dz)
-
-    def across_cores(dz):
+    for dz in range(4):
         to_partner(texts, text_plane_recv, 4, text_core_recv, dz)
+    for dz in range(4):
         to_partner(images, image_plane_recv, 5, image_core_recv, dz)
-
-    for dz in (1, 2, 3):
-        forward(dz)
-    across_cores(0)
-    for dz in (1, 2, 3):
-        across_cores(dz)
-        unpack_set(0, dz - 1)
-    unpack_set(0, 3)
+        unpack_set(texts, texts_rest, 0, dz)
+        if dz > 0:
+            unpack_set(images, images_rest, 0, dz - 1)
+    unpack_set(images, images_rest, 0, 3)
 
     scale, bias = scale_ref[()], bias_ref[()]
     half = 16 * ROWS

time: 47.6 us -> 45.9 us (0.964)
  Pallas kernels: 44.8 us -> 42.9 us
    pallas_call x1, Pallas kernels: 44.8 us -> 42.9 us  [shards(): pl.pallas_call(kernel, out_shape=jax.ShapeDtypeStruct((2, rows, width), F...]
where the time goes in v3:
time: 45.9 us; the launch traced here: 45.5 us
  Pallas kernels  42.9 us (93%)
  between operations  1.93 us (4%)
  local copies, waits for them, and re-layouts  0.66 us (1%)
    pallas_call x1, Pallas kernels, shards(): pl.pallas_call(kernel, out_shape=jax.ShapeDtypeStruct((2, rows, width), F...  42.9 us

profile of v3, /device:TPU:1, one launch (start us, length us, event | category | flops | bytes accessed | tf_op | source)
XLA Modules:
  0.0 45.5 jit_solution(5870661616758714626)
XLA Ops:
  1.9 42.9 %shard_map.59 = f32[2,12,1152]{2,1,0:T(8,128)S(1)} custom-call(f32[]{:T(128)S(6)} %copy.6.scale_ref, f32[]{:T(128)S(6)} %copy.7.bias_ref, bf16[12,1152]{1,0:T(8,128)(2,1)} %image_hbm.1, bf16[12,1152]{1,0:T(8,128)(2,1)} %text_hbm.1), custom_call_target="tpu_custom_call" | custom-call | tf_op jit(solution)/shard_map/pallas_call | solution.py:329
  44.9 0.7 %slice_bitcast_fusion = (f32[12,1152]{1,0:T(8,128)}, f32[12,1152]{1,0:T(8,128)}) fusion(f32[2,12,1152]{2,1,0:T(8,128)S(1)} %shard_map.59), kind=kLoop, calls=%fused_computation | loop fusion | bytes 221184 | tf_op jit(solution)/shard_map/squeeze | solution.py:375

commit v4 on v3

--- a/solution.py
+++ b/solution.py
@@ -208,60 +208,65 @@
     def flat(ref, lane):
         return ref[lane].reshape(half, ref.shape[-1])
 
-    def coefficients(rows, cols, col_lane):
-        logits = dot(flat(rows[0], 0), flat(cols[0], col_lane), across)
-        logits = logits + dot(flat(rows[1], 0), flat(cols[1], col_lane), across)
-        logits = scale * logits + bias
-        row = lax.broadcasted_iota(jnp.int32, logits.shape, 0)
-        col = lax.broadcasted_iota(jnp.int32, logits.shape, 1)
-        held = jnp.logical_and(row % ROWS < USED, col % ROWS < USED)
-        return logits, held, jnp.where(held, jax.nn.sigmoid(logits), 0.0).astype(BF16)
-
-    def own_coefficients(ref, rows, cols):
-        logits, held, ref[:, own] = coefficients(rows, cols, 0)
-        corner = (slice(0, ROWS), slice(0, LANES))
-        logits, held = logits[corner], held[corner]
-        row = lax.broadcasted_iota(jnp.int32, (ROWS, LANES), 0)
-        col = lax.broadcasted_iota(jnp.int32, (ROWS, LANES), 1)
-        pairs = jnp.where(row == col, -jax.nn.sigmoid(-logits), jax.nn.sigmoid(logits))
-        ref[corner] = jnp.where(held, pairs, 0.0).astype(BF16)
+    def logits_of(rows, cols, col_lane):
+        products = dot(flat(rows[0], 0), flat(cols[0], col_lane), across)
+        products = products + dot(flat(rows[1], 0), flat(cols[1], col_lane), across)
+        return scale * products + bias
+
+    def ids(shape):
+        return [lax.broadcasted_iota(jnp.int32, shape, dim) for dim in (0, 1)]
+
+    def other_coefficients(rows, cols):
+        logits = logits_of(rows, cols, 1)
+        col = ids(logits.shape)[1]
+        return jnp.where(col % ROWS < USED, jax.nn.sigmoid(logits), 0.0).astype(BF16)
 
     own, other = slice(0, half), slice(half, 2 * half)
     all_images, all_texts = (images, images_rest), (texts, texts_rest)
-    own_coefficients(image_coefs, all_images, all_texts)
-    own_coefficients(text_coefs, all_texts, all_images)
-
-    def returns(coefs, cols, dz, terms, out, into, send, recv, plane):
-        factor = coefs[4 * ROWS * dz : 4 * ROWS * (dz + 1), :]
+    logits = logits_of(all_images, all_texts, 0)
+    row, col = ids(logits.shape)
+    held = jnp.logical_and(row % ROWS < USED, col % ROWS < USED)
+    image_coefs[:, own] = jnp.where(held, jax.nn.sigmoid(logits), 0.0).astype(BF16)
+    corner = (slice(0, ROWS), slice(0, LANES))
+    logits = logits[corner]
+    row, col = ids(logits.shape)
+    pairs = jnp.where(row == col, -jax.nn.sigmoid(-logits), jax.nn.sigmoid(logits))
+    image_coefs[corner] = jnp.where(held[corner], pairs, 0.0).astype(BF16)
+    text_coefs[:, own] = image_coefs[:, own].astype(F32).T.astype(BF16)
+
+    def returns(coefs, cols, places, terms, out, into, send, recv, plane):
+        first = places[-1]
+        factor = coefs[4 * ROWS * first : 4 * ROWS * (first + 2), :]
         main, rest = (
-            dot(factor, ref[...].reshape(2 * half, ref.shape[-1]), ((1,), (0,))).reshape(4, ROWS, ref.shape[-1])
+            dot(factor, ref[...].reshape(2 * half, ref.shape[-1]), ((1,), (0,))).reshape(8, ROWS, ref.shape[-1])
             for ref in cols
         )
         packed = pack(main, rest)
-        terms[dz] = packed[0]
-        out[dz] = packed[1:4].astype(BF16)
-        for k in AROUND:
-            remote(out.at[dz, k - 1], into.at[dz, k - 1], send, recv.at[dz], plane[k]).start()
-
-    def image_returns(dz):
+        for dz in places:
+            blocks = packed[4 * (dz - first) : 4 * (dz - first + 1)]
+            terms[dz] = blocks[0]
+            out[dz] = blocks[1:4].astype(BF16)
+            for k in AROUND:
+                remote(out.at[dz, k - 1], into.at[dz, k - 1], send, recv.at[dz], plane[k]).start()
+
+    def image_returns(places):
         returns(
-            image_coefs, all_texts, dz, image_terms, image_plane_out, image_plane_in, 6, image_back_recv, image_plane
+            image_coefs, all_texts, places, image_terms, image_plane_out, image_plane_in, 6, image_back_recv, image_plane
         )
 
-    def text_returns(dz):
-        returns(text_coefs, all_images, dz, text_terms, text_plane_out, text_plane_in, 7, text_back_recv, text_plane)
+    def text_returns(places):
+        returns(text_coefs, all_images, places, text_terms, text_plane_out, text_plane_in, 7, text_back_recv, text_plane)
 
     for dz in range(4):
         partner_complete(texts, texts_rest, text_core_recv, dz)
-    image_coefs[:, other] = coefficients(all_images, all_texts, 1)[2]
-    image_returns(3)
+    image_coefs[:, other] = other_coefficients(all_images, all_texts)
+    image_returns((3, 2))
     for dz in range(4):
         partner_complete(images, images_rest, image_core_recv, dz)
-    text_coefs[:, other] = coefficients(all_texts, all_images, 1)[2]
-    text_returns(3)
-    for dz in (2, 1):
-        image_returns(dz)
-        text_returns(dz)
+    text_coefs[:, other] = other_coefficients(all_texts, all_images)
+    text_returns((3, 2))
+    image_returns((1, 0))
+    text_returns((1, 0))
 
     def summed(dz, terms, into, recv):
         arrived(into.at[dz], recv.at[dz])
@@ -281,11 +286,7 @@
         text_z_out[k - 1] = text_sum(k).astype(BF16)
         remote(text_z_out.at[k - 1], text_z_in.at[k - 1], 9, last_recv.at[1], text_z[k]).start()
 
-    image_z_return(3)
-    image_returns(0)
-    text_z_return(3)
-    text_returns(0)
-    for k in (2, 1):
+    for k in AROUND:
         image_z_return(k)
         text_z_return(k)
     for blocks, first in ((texts, 0), (images, 2)):

time: 45.9 us -> 45.7 us (level)
  no operation moved by 1% of the time
where the time goes in v4:
time: 45.7 us; the launch traced here: 45.5 us
  Pallas kernels  42.9 us (94%)
  between operations  1.93 us (4%)
  local copies, waits for them, and re-layouts  0.66 us (1%)
    pallas_call x1, Pallas kernels, shards(): pl.pallas_call(kernel, out_shape=jax.ShapeDtypeStruct((2, rows, width), F...  42.9 us

profile of v4, /device:TPU:1, one launch (start us, length us, event | category | flops | bytes accessed | tf_op | source)
XLA Modules:
  0.0 45.5 jit_solution(3410676389682439431)
XLA Ops:
  1.9 42.9 %shard_map.59 = f32[2,12,1152]{2,1,0:T(8,128)S(1)} custom-call(f32[]{:T(128)S(6)} %copy.6.scale_ref, f32[]{:T(128)S(6)} %copy.7.bias_ref, bf16[12,1152]{1,0:T(8,128)(2,1)} %image_hbm.1, bf16[12,1152]{1,0:T(8,128)(2,1)} %text_hbm.1), custom_call_target="tpu_custom_call" | custom-call | tf_op jit(solution)/shard_map/pallas_call | solution.py:330
  44.8 0.7 %slice_bitcast_fusion = (f32[12,1152]{1,0:T(8,128)}, f32[12,1152]{1,0:T(8,128)}) fusion(f32[2,12,1152]{2,1,0:T(8,128)S(1)} %shard_map.59), kind=kLoop, calls=%fused_computation | loop fusion | bytes 221184 | tf_op jit(solution)/shard_map/squeeze | solution.py:376

commit v5 on v4

--- a/solution.py
+++ b/solution.py
@@ -232,7 +232,6 @@
     row, col = ids(logits.shape)
     pairs = jnp.where(row == col, -jax.nn.sigmoid(-logits), jax.nn.sigmoid(logits))
     image_coefs[corner] = jnp.where(held[corner], pairs, 0.0).astype(BF16)
-    text_coefs[:, own] = image_coefs[:, own].astype(F32).T.astype(BF16)
 
     def returns(coefs, cols, places, terms, out, into, send, recv, plane):
         first = places[-1]
@@ -261,6 +260,7 @@
         partner_complete(texts, texts_rest, text_core_recv, dz)
     image_coefs[:, other] = other_coefficients(all_images, all_texts)
     image_returns((3, 2))
+    text_coefs[:, own] = image_coefs[:, own].astype(F32).T.astype(BF16)
     for dz in range(4):
         partner_complete(images, images_rest, image_core_recv, dz)
     text_coefs[:, other] = other_coefficients(all_texts, all_images)
@@ -286,9 +286,12 @@
         text_z_out[k - 1] = text_sum(k).astype(BF16)
         remote(text_z_out.at[k - 1], text_z_in.at[k - 1], 9, last_recv.at[1], text_z[k]).start()
 
-    for k in AROUND:
-        image_z_return(k)
-        text_z_return(k)
+    image_z_return(3)
+    image_z_return(2)
+    text_z_return(3)
+    text_z_return(2)
+    image_z_return(1)
+    text_z_return(1)
     for blocks, first in ((texts, 0), (images, 2)):
         left(blocks.at[0, 0, pl.ds(1, 3)], first)
         left(blocks.at[0, pl.ds(1, 3)], first + 1)

time: 45.7 us -> 46.2 us (1.011)
  Pallas kernels: 42.9 us -> 43.4 us
    pallas_call x1, Pallas kernels: 42.9 us -> 43.4 us  [shards(): pl.pallas_call(kernel, out_shape=jax.ShapeDtypeStruct((2, rows, width), F...]
where the time goes in v5:
time: 46.2 us; the launch traced here: 46 us
  Pallas kernels  43.4 us (94%)
  between operations  1.93 us (4%)
  local copies, waits for them, and re-layouts  0.66 us (1%)
    pallas_call x1, Pallas kernels, shards(): pl.pallas_call(kernel, out_shape=jax.ShapeDtypeStruct((2, rows, width), F...  43.4 us

profile of v5, /device:TPU:1, one launch (start us, length us, event | category | flops | bytes accessed | tf_op | source)
XLA Modules:
  0.0 46.0 jit_solution(3599246169530900641)
XLA Ops:
  1.9 43.4 %shard_map.59 = f32[2,12,1152]{2,1,0:T(8,128)S(1)} custom-call(f32[]{:T(128)S(6)} %copy.6.scale_ref, f32[]{:T(128)S(6)} %copy.7.bias_ref, bf16[12,1152]{1,0:T(8,128)(2,1)} %image_hbm.1, bf16[12,1152]{1,0:T(8,128)(2,1)} %text_hbm.1), custom_call_target="tpu_custom_call" | custom-call | tf_op jit(solution)/shard_map/pallas_call | solution.py:333
  45.3 0.7 %slice_bitcast_fusion = (f32[12,1152]{1,0:T(8,128)}, f32[12,1152]{1,0:T(8,128)}) fusion(f32[2,12,1152]{2,1,0:T(8,128)S(1)} %shard_map.59), kind=kLoop, calls=%fused_computation | loop fusion | bytes 221184 | tf_op jit(solution)/shard_map/squeeze | solution.py:379

commit v6 on v5

--- a/solution.py
+++ b/solution.py
@@ -31,15 +31,15 @@
     def other_core(self):
         return self.at(self.x, self.y, self.z, 1 - self.core)
 
-    def text_plane(self, k):
+    def text_plane(self, k, lane=0):
         x = self.x + (k % 2) * (1 - 2 * (self.x % 2))
         y = self.y + (k // 2) * (1 - 2 * (self.y % 2))
-        return self.at(x, y, self.z, self.core)
-
-    def image_plane(self, k):
+        return self.at(x, y, self.z, self.core + lane * (1 - 2 * self.core))
+
+    def image_plane(self, k, lane=0):
         x = (self.x + (k % 2) * (2 * (self.x % 2) + 3)) % 4
         y = (self.y + (k // 2) * (2 * (self.y % 2) + 3)) % 4
-        return self.at(x, y, self.z, self.core)
+        return self.at(x, y, self.z, self.core + lane * (1 - 2 * self.core))
 
     def text_z(self, k):
         z = self.z + (k % 2) * (1 - 2 * (self.z % 2)) + (k // 2) * (4 - 8 * ((self.z // 4) % 2))
@@ -131,9 +131,10 @@
     text_plane, image_plane, image_z, text_z = (
         {k: way(k) for k in AROUND} for way in (place.text_plane, place.image_plane, place.image_z, place.text_z)
     )
+    text_across, image_across = ({k: way(k, 1) for k in AROUND} for way in (place.text_plane, place.image_plane))
     barrier = pltpu.get_barrier_semaphore()
     for k in AROUND:
-        for device in (text_z[k], image_z[k], text_plane[k], image_plane[k]):
+        for device in (text_z[k], image_z[k], text_plane[k], image_plane[k], text_across[k], image_across[k]):
             pl.semaphore_signal(barrier, inc=1, device_id=device, device_id_type=MESH)
     pl.semaphore_signal(barrier, inc=1, device_id=partner, device_id_type=MESH)
     units[...] = jnp.zeros_like(units)
@@ -147,7 +148,7 @@
     own_packed = pack(own[:, :, :MAIN], own_rest).astype(BF16)
     images[0, 0, 0] = own_packed[0]
     texts[0, 0, 0] = own_packed[1]
-    pl.semaphore_wait(barrier, 13)
+    pl.semaphore_wait(barrier, 19)
 
     def remote(src, dst, send, recv, device):
         return pltpu.make_async_remote_copy(
@@ -171,7 +172,8 @@
 
     def to_partner(blocks, plane_recv, send, core_recv, dz):
         arrived(blocks.at[0, dz, pl.ds(1, 3)], plane_recv.at[dz])
-        remote(blocks.at[0, dz], blocks.at[1, dz], send, core_recv.at[dz], partner).start()
+        if dz > 0:
+            remote(blocks.at[0, dz], blocks.at[1, dz], send, core_recv.at[dz], partner).start()
 
     def unpack_set(blocks, rests, lane, dz):
         rests[lane, dz] = unpack_rest(blocks[lane, dz].astype(F32)).astype(BF16)
@@ -186,6 +188,13 @@
         remote(images.at[0, 0, 0], images.at[0, k, 0], 2, image_z_recv.at[k], image_z[k]).start()
     spread(texts, text_plane, 1, text_plane_recv, 0)
     spread(images, image_plane, 3, image_plane_recv, 0)
+
+    for i, (blocks, across_plane, recv) in enumerate(
+        ((texts, text_across, text_core_recv), (images, image_across, image_core_recv))
+    ):
+        for k in AROUND:
+            remote(blocks.at[0, 0, 0], blocks.at[1, 0, k], 10 + i, recv.at[0], across_plane[k]).start()
+        remote(blocks.at[0, 0, 0], blocks.at[1, 0, 0], 12 + i, recv.at[0], partner).start()
     for dz in (1, 2, 3):
         arrived(texts.at[0, dz, 0], text_z_recv.at[dz])
         spread(texts, text_plane, 1, text_plane_recv, dz)
@@ -295,7 +304,9 @@
     for blocks, first in ((texts, 0), (images, 2)):
         left(blocks.at[0, 0, pl.ds(1, 3)], first)
         left(blocks.at[0, pl.ds(1, 3)], first + 1)
-        left(blocks.at[0], first // 2 + 4)
+        left(blocks.at[0, pl.ds(1, 3)], first // 2 + 4)
+        left(blocks.at[0, 0, pl.ds(1, 3)], first // 2 + 10)
+        left(blocks.at[0, 0, 0], first // 2 + 12)
     image_total = image_sum(0)
     text_total = text_sum(0)
     left(image_plane_out, 6)
@@ -356,7 +367,7 @@
             half(3),
             half(3),
             dma(2),
-            dma(10),
+            dma(14),
             dma(4),
             dma(4),
             dma(4),

time: 46.2 us -> 46.1 us (level)
  the two profiles are of different devices: /device:TPU:1 before, /device:TPU:32 now
where the time goes in v6:
time: 46.1 us; the launch traced here: 45.9 us
  Pallas kernels  43.3 us (94%)
  between operations  1.93 us (4%)
  local copies, waits for them, and re-layouts  0.66 us (1%)
    pallas_call x1, Pallas kernels, shards(): pl.pallas_call(kernel, out_shape=jax.ShapeDtypeStruct((2, rows, width), F...  43.3 us

profile of v6, /device:TPU:32, one launch (start us, length us, event | category | flops | bytes accessed | tf_op | source)
XLA Modules:
  0.0 45.9 jit_solution(15097777455590396270)
XLA Ops:
  1.9 43.3 %shard_map.59 = f32[2,12,1152]{2,1,0:T(8,128)S(1)} custom-call(f32[]{:T(128)S(6)} %copy.6.scale_ref, f32[]{:T(128)S(6)} %copy.7.bias_ref, bf16[12,1152]{1,0:T(8,128)(2,1)} %image_hbm.1, bf16[12,1152]{1,0:T(8,128)(2,1)} %text_hbm.1), custom_call_target="tpu_custom_call" | custom-call | tf_op jit(solution)/shard_map/pallas_call | solution.py:344
  45.3 0.7 %slice_bitcast_fusion = (f32[12,1152]{1,0:T(8,128)}, f32[12,1152]{1,0:T(8,128)}) fusion(f32[2,12,1152]{2,1,0:T(8,128)S(1)} %shard_map.59), kind=kLoop, calls=%fused_computation | loop fusion | bytes 221184 | tf_op jit(solution)/shard_map/squeeze | solution.py:390

commit v7 on v4

--- a/solution.py
+++ b/solution.py
@@ -180,9 +180,9 @@
         arrived(blocks.at[1, dz], core_recv.at[dz])
         unpack_set(blocks, rests, 1, dz)
 
-    for k in AROUND:
+    for k in (1, 2, 3):
         remote(texts.at[0, 0, 0], texts.at[0, k, 0], 0, text_z_recv.at[k], text_z[k]).start()
-    for k in AROUND:
+    for k in (1, 2, 3):
         remote(images.at[0, 0, 0], images.at[0, k, 0], 2, image_z_recv.at[k], image_z[k]).start()
     spread(texts, text_plane, 1, text_plane_recv, 0)
     spread(images, image_plane, 3, image_plane_recv, 0)

time: 45.7 us -> 45.4 us (level); the launches traced: 45.5 us -> 44.6 us
  Pallas kernels: 42.9 us -> 42 us
    pallas_call x1, Pallas kernels: 42.9 us -> 42 us  [shards(): pl.pallas_call(kernel, out_shape=jax.ShapeDtypeStruct((2, rows, width), F...]
where the time goes in v7:
time: 45.4 us; the launch traced here: 44.6 us
  Pallas kernels  42 us (93%)
  between operations  1.93 us (4%)
  local copies, waits for them, and re-layouts  0.66 us (1%)
    pallas_call x1, Pallas kernels, shards(): pl.pallas_call(kernel, out_shape=jax.ShapeDtypeStruct((2, rows, width), F...  42 us

profile of v7, /device:TPU:1, one launch (start us, length us, event | category | flops | bytes accessed | tf_op | source)
XLA Modules:
  0.0 44.6 jit_solution(13853983454266390775)
XLA Ops:
  1.9 42.0 %shard_map.59 = f32[2,12,1152]{2,1,0:T(8,128)S(1)} custom-call(f32[]{:T(128)S(6)} %copy.6.scale_ref, f32[]{:T(128)S(6)} %copy.7.bias_ref, bf16[12,1152]{1,0:T(8,128)(2,1)} %image_hbm.1, bf16[12,1152]{1,0:T(8,128)(2,1)} %text_hbm.1), custom_call_target="tpu_custom_call" | custom-call | tf_op jit(solution)/shard_map/pallas_call | solution.py:330
  43.9 0.7 %slice_bitcast_fusion = (f32[12,1152]{1,0:T(8,128)}, f32[12,1152]{1,0:T(8,128)}) fusion(f32[2,12,1152]{2,1,0:T(8,128)S(1)} %shard_map.59), kind=kLoop, calls=%fused_computation | loop fusion | bytes 221184 | tf_op jit(solution)/shard_map/squeeze | solution.py:376

commit v8 on v5

--- a/solution.py
+++ b/solution.py
@@ -180,9 +180,9 @@
         arrived(blocks.at[1, dz], core_recv.at[dz])
         unpack_set(blocks, rests, 1, dz)
 
-    for k in AROUND:
+    for k in (1, 2, 3):
         remote(texts.at[0, 0, 0], texts.at[0, k, 0], 0, text_z_recv.at[k], text_z[k]).start()
-    for k in AROUND:
+    for k in (1, 2, 3):
         remote(images.at[0, 0, 0], images.at[0, k, 0], 2, image_z_recv.at[k], image_z[k]).start()
     spread(texts, text_plane, 1, text_plane_recv, 0)
     spread(images, image_plane, 3, image_plane_recv, 0)

time: 46.2 us -> 45.4 us (0.983)
  the two profiles are of different devices: /device:TPU:1 before, /device:TPU:32 now
where the time goes in v8:
time: 45.4 us; the launch traced here: 45.2 us
  Pallas kernels  42.6 us (94%)
  between operations  1.93 us (4%)
  local copies, waits for them, and re-layouts  0.66 us (1%)
    pallas_call x1, Pallas kernels, shards(): pl.pallas_call(kernel, out_shape=jax.ShapeDtypeStruct((2, rows, width), F...  42.6 us

profile of v8, /device:TPU:32, one launch (start us, length us, event | category | flops | bytes accessed | tf_op | source)
XLA Modules:
  0.0 45.2 jit_solution(6984144355540453017)
XLA Ops:
  1.9 42.6 %shard_map.59 = f32[2,12,1152]{2,1,0:T(8,128)S(1)} custom-call(f32[]{:T(128)S(6)} %copy.6.scale_ref, f32[]{:T(128)S(6)} %copy.7.bias_ref, bf16[12,1152]{1,0:T(8,128)(2,1)} %image_hbm.1, bf16[12,1152]{1,0:T(8,128)(2,1)} %text_hbm.1), custom_call_target="tpu_custom_call" | custom-call | tf_op jit(solution)/shard_map/pallas_call | solution.py:333
  44.5 0.7 %slice_bitcast_fusion = (f32[12,1152]{1,0:T(8,128)}, f32[12,1152]{1,0:T(8,128)}) fusion(f32[2,12,1152]{2,1,0:T(8,128)S(1)} %shard_map.59), kind=kLoop, calls=%fused_computation | loop fusion | bytes 221184 | tf_op jit(solution)/shard_map/squeeze | solution.py:379
